TPU v7x, 32 devices: a whole 2x2x4 slice. The times are simulated.
32 devices in a mesh: grp: 4 (over y, core), sub: 8 (over z, x).
Axes of the slice: x: 2, y: 2, z: 4, core: 2. Of those that a mesh axis runs over, the one named last changes fastest.
Arguments:
- deflation: bfloat16 [32, 131072], P(None, ('grp', 'sub'))
- operator_blocks: bfloat16 [12288, 4096], P(('grp', 'sub'))
- diagonal: float32 [131072], P(('grp', 'sub'))
- block_rows: int32 [32, 384], P(('grp', 'sub')), may hold values from 0 to 63
- block_cols: int32 [32, 384], P(('grp', 'sub')), may hold values from 0 to 127, as said below
- live_count: int32 [32], P(('grp', 'sub')), may hold values from 96 to 384, as said below
- send_blocks: int32 [32, 4, 16], P(('grp', 'sub')), may hold values from 0 to 63
- residual: float32 [131072], P(('grp', 'sub')), may hold values from -6 to 6
Outputs:
- correction: float32 [131072], P(('grp', 'sub'))
- coarse_rows: float32 [32, 5120], P(('grp', 'sub'))
Inputs may be any that keep to these rules, and one draw needn't show every extreme that they name: Slots from live_count on are padding and do not act; some subdomain uses all 384 slots and some uses exactly the least. `block_cols`: an even slot's column is below 64, the subdomain's own node block; an odd slot b's column lies in ghost region (b mod 8 + 1) / 2 - 1 of step one, numbered 0 to 3, each of 16 ghost blocks from 64 on. Several slots may share a position. `send_blocks`: A node block may be listed more than once.
All inputs are finite; a program needn't handle non-finite values.
Results may differ from a plain program's by a relative error of at most 0.00045.
Values may be sent and summed in bfloat16 or wider, within the bound.
A program may use at most 128 MiB of HBM per device.

v0:
```python
import math

import jax
import jax.numpy as jnp
from jax import lax
from jax.sharding import PartitionSpec as P

NV = 32
BS = 64
NODES = 64
SEND = 16
EXT = 128
BLK = 384
ROWS = 4096


HIGHEST_PREC = lax.Precision.HIGHEST


def passed_along(value, axis, steps):
    count = lax.axis_size(axis)
    pairs = [(source, (source + steps) % count) for source in range(count)]
    return lax.ppermute(value, axis, pairs)


def from_behind(value, axis, steps):
    count = lax.axis_size(axis)
    initial, last = (max(0, -steps), min(count, count - steps))
    return lax.ppermute(value, axis, [(source, source + steps) for source in range(initial, last)])


def split_parts(values):
    upper = values.astype(jnp.bfloat16)
    lower = (values - upper.astype(jnp.float32)).astype(jnp.bfloat16)
    return (upper, lower)


def per_device(
    deflation, operator_blocks, diagonal, block_rows, block_cols, live_count, send_blocks, residual
):
    node_tiles = deflation.reshape(NV, NODES, BS)
    rim_width = SEND * BS

    def outgoing(region):
        return jnp.take(node_tiles, send_blocks[0, region], axis=1).reshape(NV, rim_width)

    to_next = outgoing(0)
    to_prev = outgoing(1)
    to_upper = outgoing(2)
    to_lower = outgoing(3)
    from_prev = passed_along(to_next, "sub", 1)
    from_next = passed_along(to_prev, "sub", -1)
    from_lower = from_behind(to_upper, "grp", 1)
    from_upper = from_behind(to_lower, "grp", -1)
    extended = jnp.concatenate(
        [deflation, from_prev, from_next, from_lower, from_upper], axis=1
    ).reshape(NV, EXT, BS)
    col_all = block_cols[0]
    owners = jnp.where(col_all < NODES, 0, 1 + (col_all - NODES) // SEND)
    segment = owners * NODES + block_rows[0]
    live_mask = (lax.iota(jnp.int32, BLK) < live_count[0]).astype(jnp.float32)

    def contribute(first_slot, slot_count):
        col_ids = lax.dynamic_slice_in_dim(col_all, first_slot, slot_count)
        picked = jnp.take(extended, col_ids, axis=1)
        block_mats = lax.dynamic_slice_in_dim(operator_blocks, first_slot, slot_count, 0).reshape(
            slot_count, BS, BS
        )
        products = jnp.einsum(
            "bij,vbj->bvi", block_mats, picked, preferred_element_type=jnp.float32
        )
        seg_part = lax.dynamic_slice_in_dim(segment, first_slot, slot_count)
        live_part = lax.dynamic_slice_in_dim(live_mask, first_slot, slot_count)
        return jax.ops.segment_sum(
            products * live_part[:, None, None], seg_part, num_segments=5 * NODES
        )

    group_size = math.gcd(BLK, 64)
    loop_turns = (live_count[0] + group_size - 1) // group_size

    def add_group(turn, total):
        return total + contribute(turn * group_size, group_size)

    summed = lax.fori_loop(0, loop_turns, add_group, jnp.zeros((5 * NODES, NV, BS), jnp.float32))
    own_float = deflation.astype(jnp.float32)
    applied = summed.reshape(5, NODES, NV, BS)
    applied_hi, applied_lo = split_parts(applied)
    coarse_rows = jnp.einsum(
        "vni,onwi->ovw", node_tiles, applied_hi, preferred_element_type=jnp.float32
    )
    coarse_rows = coarse_rows + jnp.einsum(
        "vni,onwi->ovw", node_tiles, applied_lo, preferred_element_type=jnp.float32
    )
    scaled = diagonal.reshape(1, NODES, BS) * own_float.reshape(NV, NODES, BS)
    scaled_hi, scaled_lo = split_parts(scaled)
    diag_block = jnp.einsum(
        "vni,wni->vw", node_tiles, scaled_hi, preferred_element_type=jnp.float32
    )
    diag_block = diag_block + jnp.einsum(
        "vni,wni->vw", node_tiles, scaled_lo, preferred_element_type=jnp.float32
    )
    coarse_rows = coarse_rows.at[0].add(diag_block) / ROWS
    coarse_rhs = jnp.dot(own_float, residual, precision=HIGHEST_PREC) / 64.0
    cycle_size = lax.axis_size("sub")
    sub_index = lax.axis_index("sub")
    targets = jnp.stack([sub_index, (sub_index - 1) % cycle_size, (sub_index + 1) % cycle_size])
    one_hot_cols = (lax.iota(jnp.int32, cycle_size)[None, :] == targets[:, None]).astype(
        jnp.float32
    )
    strip = jnp.einsum(
        "ovw,ot->vtw", coarse_rows[:3], one_hot_cols, precision=HIGHEST_PREC
    ).reshape(NV, cycle_size * NV)
    coarse_full, gathered_rhs = (
        lax.all_gather(strip, "sub", axis=0, tiled=True),
        lax.all_gather(coarse_rhs, "sub", axis=0, tiled=True),
    )
    symmetric = (coarse_full + coarse_full.T) * 0.5
    factor_low = jnp.linalg.cholesky(symmetric)
    solved = jax.scipy.linalg.cho_solve((factor_low, True), gathered_rhs)
    own_part = lax.dynamic_slice_in_dim(solved, sub_index * NV, NV)
    correction = jnp.dot(own_part, own_float, precision=HIGHEST_PREC)
    return (correction, coarse_rows.reshape(1, 5 * NV * NV))


def solution(mesh):
    placed = (
        P(None, ("grp", "sub")),
        P(("grp", "sub"), None),
        P(("grp", "sub")),
        P(("grp", "sub"), None),
        P(("grp", "sub"), None),
        P(("grp", "sub")),
        P(("grp", "sub"), None, None),
        P(("grp", "sub")),
    )
    return jax.shard_map(
        per_device,
        mesh=mesh,
        in_specs=placed,
        out_specs=(P(("grp", "sub")), P(("grp", "sub"), None)),
        check_vma=False,
    )
```

profile of v0, /device:TPU:4, one launch (start us, length us, event | category | flops | bytes accessed | tf_op | source)
XLA Modules:
  0.0 231.1 jit_solution(13607523804885360231)
XLA Ops:
  0.7 0.8 compare_and_fusion.1
  1.5 1.5 reshape.133
  3.0 0.3 copy.58
  3.4 0.6 gather_fusion.1
  4.0 0.6 gather_fusion.2
  4.7 0.1 reshape.134
  4.9 1.5 collective-permute-start
  6.5 0.1 reshape.135
  6.6 3.3 %collective-permute-start.1 = (bf16[32,1024]{1,0:T(8,128)(2,1)S(1)}, bf16[32,1024]{1,0:T(8,128)(2,1)S(1)}, u32[]{:S(2)}, u32[]{:S(2)}) collective-permute-start(bf16[32,1024]{1,0:T(8,128)(2,1)S(1)} %reshape.135), channel_id=1, source_target_pairs={{0,7},{1,0},{2,1},{3,2},{4,3},{5,4},{6,5},{7,6},{8,15},{9,8},{10,9... | collective-permute-start | bytes 196616 | tf_op jit(solution)/shard_map/ppermute | solution.py:23
  9.9 0.6 gather_fusion.3
  10.5 0.6 gather_fusion.4
  11.4 1.9 collective-permute-start.2
  13.5 3.6 %collective-permute-start.3 = (bf16[32,1024]{1,0:T(8,128)(2,1)S(1)}, bf16[32,1024]{1,0:T(8,128)(2,1)S(1)}, u32[]{:S(2)}, u32[]{:S(2)}) collective-permute-start(bf16[32,1024]{1,0:T(8,128)(2,1)S(1)} %reshape.137), channel_id=1, source_target_pairs={{8,0},{16,8},{24,16},{9,1},{17,9},{25,17},{10,2},{18,10},{26,18},{... | collective-permute-start | bytes 196616 | tf_op jit(solution)/shard_map/ppermute | solution.py:29
  17.9 0.8 copy.68
  18.9 0.3 fusion.24
  19.2 0.8 copy.73
  19.9 1.5 copy.71
  21.5 0.3 fusion.23
  21.8 0.7 dynamic-slice.12
  23.1 0.2 dynamic-update-slice.14
  23.3 18.9 %all-reduce.1 = f32[256]{0:T(256)S(1)} all-reduce(f32[256]{0:T(256)S(1)} %dynamic-update-slice.14), channel_id=1, replica_groups=mesh['grp'=4,'sub'=8] {'sub'}, use_global_device_ids=true, to_apply=%add.1 | all-reduce | flops 256 | bytes 2048
  42.3 0.3 convolution_bitcast_fusion.1
  42.7 1.1 reshape.138
  43.9 1.7 copy.66
  45.6 3.0 %broadcast.187 = f32[320,32,64]{2,1,0:T(8,128)} broadcast(f32[]{:T(128)} %constant.205.clone.1), dimensions={} | broadcast | bytes 2621444 | tf_op jit(solution)/shard_map/broadcast.12
  48.6 26.2 %while.12 = (s32[]{:T(128)}, f32[320,32,64]{2,1,0:T(8,128)}, s32[]{:T(128)}, s32[384]{0:T(512)S(1)}, s32[384]{0:T(512)S(1)}, /*index=5*/bf16[32,128,64]{2,0,1:T(...) while((s32[]{:T(128)}, f32[320,32,64]{2,1,0:T(8,128)}, ...), condition=%wide.region_2.4_spmd, body=%wide.region_0.3_spmd.sunk | while | flops 17171844 | bytes 5511987 | solution.py:84
  48.6 1.9 gather_fusion
  50.5 1.1 constant_dynamic-slice_fusion.4
  51.6 1.1 reshape.271
  52.8 0.7 convolution_multiply_fusion.2
  53.6 8.0 %scatter_fusion = f32[320,32,64]{2,1,0:T(8,128)} fusion(f32[320,32,64]{2,1,0:T(8,128)} %get-tuple-element.241, s32[64]{0:T(128)S(1)} %dynamic_slice.36, f32[64,32,64]{2,1,0:T(8,128)S(1)} %convolution_multiply_fusion.2), kind=kCustom, calls=%fused_computation.5.clone.1 | custom fusion | flops 131072 | bytes 1573120 | tf_op jit(solution)/shard_map/while/body/scatter-add | solution.py:74
  61.7 1.9 gather_fusion
  63.6 1.1 constant_dynamic-slice_fusion.4
  64.7 1.1 reshape.271
  65.9 0.7 convolution_multiply_fusion.2
  66.7 8.1 %scatter_fusion = f32[320,32,64]{2,1,0:T(8,128)} fusion(f32[320,32,64]{2,1,0:T(8,128)} %get-tuple-element.241, s32[64]{0:T(128)S(1)} %dynamic_slice.36, f32[64,32,64]{2,1,0:T(8,128)S(1)} %convolution_multiply_fusion.2), kind=kCustom, calls=%fused_computation.5.clone.1 | custom fusion | flops 131072 | bytes 1573120 | tf_op jit(solution)/shard_map/while/body/scatter-add | solution.py:74
  74.8 6.2 %copy.67 = f32[5,64,32,64]{1,2,3,0:T(8,128)} copy(f32[5,64,32,64]{3,2,1,0:T(8,128)} %bitcast.168) | data formatting | bytes 5242880 | tf_op jit(solution)/shard_map/reshape | solution.py:86
  80.9 3.5 %fusion.9 = f32[5,32,32]{2,1,0:T(8,128)S(1)} fusion(f32[5,64,32,64]{1,2,3,0:T(8,128)} %copy.67, bf16[32,64,64]{1,0,2:T(8,128)(2,1)S(1)} %copy.68), kind=kOutput, calls=%fused_computation.24 | convolution fusion | flops 42598400 | bytes 2904064 | tf_op jit(solution)/shard_map/vni,onwi->ovw/dot_general | solution.py:88
  84.4 0.6 copy-done.1
  85.0 0.8 fusion.14
  85.8 0.3 fusion.18
  86.2 0.3 convolution_bitcast_fusion
  86.6 78.6 %all_gather.6 = f32[256,256]{1,0:T(8,128)S(1)} all-gather(f32[32,256]{1,0:T(8,128)S(1)} %reshape.142), channel_id=1, replica_groups=mesh['grp'=4,'sub'=8] {'sub'}, dimensions={0}, use_global_device_ids=true | all-gather | bytes 294912 | tf_op jit(solution)/shard_map/all_gather | solution.py:114
  165.6 11.7 %cholesky.50 = f32[128,128]{1,0:T(8,128)S(1)} custom-call(f32[128,128]{1,0:T(8,128)S(1)} %cholesky.118), custom_call_target="Cholesky" | custom-call | tf_op jit(solution)/shard_map/jit(cholesky)/cholesky | solution.py:118
  177.5 9.8 %custom-call.18 = f32[1,128,128]{1,2,0:T(8,128)S(1)} custom-call(f32[1,128,128]{2,1,0:T(8,128)S(1)} %get-tuple-element.132), custom_call_target="InvertDiagBlocksLowerTriangular" | custom-call | tf_op jit(solution)/shard_map/jit(cholesky)/cholesky | solution.py:118
  187.3 0.2 constant_dynamic-update-slice_fusion.5
  187.5 0.3 convolution_subtract_fusion
  187.8 11.7 %cholesky.105 = f32[128,128]{1,0:T(8,128)S(1)} custom-call(f32[128,128]{1,0:T(8,128)S(1)} %convolution_subtract_fusion), custom_call_target="Cholesky" | custom-call | tf_op jit(solution)/shard_map/jit(cholesky)/cholesky | solution.py:118
  199.5 0.7 compare_reduce_fusion
  200.2 0.6 compare_reduce_fusion.1
  202.3 5.5 %while.13 = (s32[]{:T(128)}, f32[256,256]{1,0:T(8,128)S(1)}, s32[2,2]{1,0:T(2,128)S(1)}, f32[2,128,128]{2,1,0:T(8,128)}, s32[]{:T(128)}) while((s32[]{:T(128)}, f32[256,256]{1,0:T(8,128)S(1)}, s32[2,2]{1,0:T(2,128)S(1)}, f32[2,128,128]{2,1,0:T(8,128)}, s32[]{:T(128)}) %tuple.66), condition=%wide.while_cond.1, body=%wide.while_body.1.sunk | while | flops 2 | bytes 132705 | solution.py:119
  202.5 0.6 fusion.73
  203.1 2.0 bitcast_dynamic-update-slice_fusion.2
  205.2 0.6 fusion.73
  205.8 2.1 bitcast_dynamic-update-slice_fusion.2
  207.8 20.5 %custom-call.19 = f32[2,128,128]{1,2,0:T(8,128)S(1)} custom-call(f32[2,128,128]{2,1,0:T(8,128)} %get-tuple-element.66), custom_call_target="InvertDiagBlocksLowerTriangular" | custom-call | tf_op jit(solution)/shard_map/jit(_cho_solve)/triangular_solve | solution.py:119
  228.3 0.2 fusion.32
  228.5 0.2 fusion.22
  228.7 0.2 convolution_bitcast_fusion.6
  228.9 0.2 convolution_bitcast_fusion.5
  229.1 0.2 fusion.20
  229.3 0.2 convolution_bitcast_fusion.3
  229.5 0.8 reshape.143
  230.2 0.9 fusion.46
  (70 shorter events, 2.4 us)
Async XLA Ops:
  0.6 20.8 %copy-start = (f32[4096]{0:T(1024)S(1)}, f32[4096]{0:T(1024)}, u32[]{:S(2)}) copy-start(f32[4096]{0:T(1024)} %param.21) | copy-start | bytes 49156
  0.6 16.5 %copy-start.2 = (bf16[32,4096]{1,0:T(8,128)(2,1)S(1)}, bf16[32,4096]{1,0:T(8,128)(2,1)}, u32[]{:S(2)}) copy-start(bf16[32,4096]{1,0:T(8,128)(2,1)} %param.14) | copy-start | bytes 786436
  0.7 18.1 %copy-start.5 = (s32[1,384]{1,0:T(1,128)S(1)}, s32[1,384]{1,0:T(1,128)}, u32[]{:S(2)}) copy-start(s32[1,384]{1,0:T(1,128)} %param.18) | copy-start | bytes 4612
  0.7 18.1 %copy-start.6 = (s32[1,384]{1,0:T(1,128)S(1)}, s32[1,384]{1,0:T(1,128)}, u32[]{:S(2)}) copy-start(s32[1,384]{1,0:T(1,128)} %param.17) | copy-start | bytes 4612
  0.7 18.1 %copy-start.4 = (f32[4096]{0:T(1024)S(1)}, f32[4096]{0:T(1024)}, u32[]{:S(2)}) copy-start(f32[4096]{0:T(1024)} %param.16) | copy-start | bytes 49156
  3.0 18.8 %copy-start.7 = (u32[32]{0:T(128)S(1)}, u32[32]{0:T(128)}, u32[]{:S(2)}) copy-start(u32[32]{0:T(128)} %constant.242) | copy-start | bytes 388
  4.9 37.8 %collective-permute-start = (bf16[32,1024]{1,0:T(8,128)(2,1)S(1)}, bf16[32,1024]{1,0:T(8,128)(2,1)S(1)}, u32[]{:S(2)}, u32[]{:S(2)}) collective-permute-start(bf16[32,1024]{1,0:T(8,128)(2,1)S(1)} %reshape.134), channel_id=1, source_target_pairs={{0,1},{1,2},{2,3},{3,4},{4,5},{5,6},{6,7},{7,0},{8,9},{9,10},{10,1... | collective-permute-start | bytes 196616 | tf_op jit(solution)/shard_map/ppermute | solution.py:23
  6.6 36.1 %collective-permute-start.1 = (bf16[32,1024]{1,0:T(8,128)(2,1)S(1)}, bf16[32,1024]{1,0:T(8,128)(2,1)S(1)}, u32[]{:S(2)}, u32[]{:S(2)}) collective-permute-start(bf16[32,1024]{1,0:T(8,128)(2,1)S(1)} %reshape.135), channel_id=1, source_target_pairs={{0,7},{1,0},{2,1},{3,2},{4,3},{5,4},{6,5},{7,6},{8,15},{9,8},{10,9... | collective-permute-start | bytes 196616 | tf_op jit(solution)/shard_map/ppermute | solution.py:23
  11.4 31.3 %collective-permute-start.2 = (bf16[32,1024]{1,0:T(8,128)(2,1)S(1)}, bf16[32,1024]{1,0:T(8,128)(2,1)S(1)}, u32[]{:S(2)}, u32[]{:S(2)}) collective-permute-start(bf16[32,1024]{1,0:T(8,128)(2,1)S(1)} %reshape.136), channel_id=1, source_target_pairs={{0,8},{8,16},{16,24},{1,9},{9,17},{17,25},{2,10},{10,18},{18,26},{... | collective-permute-start | bytes 196616 | tf_op jit(solution)/shard_map/ppermute | solution.py:29
  13.5 29.2 %collective-permute-start.3 = (bf16[32,1024]{1,0:T(8,128)(2,1)S(1)}, bf16[32,1024]{1,0:T(8,128)(2,1)S(1)}, u32[]{:S(2)}, u32[]{:S(2)}) collective-permute-start(bf16[32,1024]{1,0:T(8,128)(2,1)S(1)} %reshape.137), channel_id=1, source_target_pairs={{8,0},{16,8},{24,16},{9,1},{17,9},{25,17},{10,2},{18,10},{26,18},{... | collective-permute-start | bytes 196616 | tf_op jit(solution)/shard_map/ppermute | solution.py:29
  80.9 4.0 %copy-start.1 = (f32[5,64,32,64]{1,2,3,0:T(8,128)S(1)}, f32[5,64,32,64]{1,2,3,0:T(8,128)}, u32[]{:S(2)}) copy-start(f32[5,64,32,64]{1,2,3,0:T(8,128)} %copy.67) | copy-start | bytes 7864324
  80.9 4.9 %copy-start.3 = (bf16[32,64,64]{1,0,2:T(8,128)(2,1)S(1)}, bf16[32,64,64]{1,0,2:T(8,128)(2,1)}, u32[]{:S(2)}) copy-start(bf16[32,64,64]{1,0,2:T(8,128)(2,1)} %copy.71) | copy-start | bytes 786436
where the time goes:
time: 234 us; the launch traced here: 231 us
  blocking collectives  97.5 us (42%)
  other arithmetic  73 us (31%)
  local copies, waits for them, and re-layouts  36.8 us (16%)
  starting transfers between devices  10.4 us (4%)
  matrix products  9.4 us (4%)
  between operations  3.78 us (2%)
    all_gather x1, blocking collectives, per_device(): lax.all_gather(strip, 'sub', axis=0, tiled=True)  78.6 us
    another operation x7, other arithmetic, per_device(): factor_low = jnp.linalg.cholesky(symmetric)  34.7 us
    another operation x3, other arithmetic, per_device(): solved = jax.scipy.linalg.cho_solve((factor_low, True), gathered_rhs)  20.5 us
    unnamed x1, blocking collectives  18.9 us
    scatter-add x2, other arithmetic, contribute(): jax.ops.segment_sum(products * live_part[:, None, None], seg_part, num_se...  16.1 us
    another operation x7, local copies, waits for them, and re-layouts  8.29 us
    reshape x1, local copies, waits for them, and re-layouts, per_device(): applied = summed.reshape(5, NODES, NV, BS)  6.15 us
    ppermute x2, starting transfers between devices, from_behind(): lax.ppermute(value, axis, [(source, source + steps) for source in range(i...  5.56 us
  transfers between devices with their start and end apart: 4, of which 0 were waited for; matrix products, arithmetic and copies ran while one was open for 3% of the time, Pallas kernels for 0%

commit v1 on v0

v1 whole, which is shorter than its diff:
```python
import functools

import jax
import jax.numpy as jnp
from jax import lax
from jax.experimental import pallas as pl
from jax.experimental.pallas import tpu as pltpu
from jax.sharding import PartitionSpec as P

NV = 32
BS = 64
NODES = 64
SEND = 16
BLK = 384
ROWS = 4096
LANES = 128
CHUNKS = ROWS // LANES
GROUP = 16
TURNS = BLK // GROUP
PARTS = 4

HIGHEST_PREC = lax.Precision.HIGHEST
MESH = pl.DeviceIdType.MESH
F32 = jnp.float32
BF16 = jnp.bfloat16


def dot_nt(a, b):
    return lax.dot_general(a, b, (((1,), (1,)), ((), ())), preferred_element_type=F32)


def hi_lo(values):
    upper = values.astype(BF16)
    lower = (values - upper.astype(F32)).astype(BF16)
    return jnp.concatenate([upper, lower], axis=0)


def assemble_kernel(
    n_grp, n_sub,
    rows_s, cols_s, live_s, send_s, z_ref, diag_ref, res_ref, a_hbm,
    strips, blocks,
    a_v, zs, zl, xn, out_b, ghost, wide, qs, strip, acc_own, acc_ghost,
    a_sem, ghost_send, ghost_recv, strip_send, strip_recv,
):
    grp = lax.axis_index("grp")
    sub = lax.axis_index("sub")
    following = lax.rem(sub + 1, n_sub)
    previous = lax.rem(sub + n_sub - 1, n_sub)
    has_lower = grp > 0
    has_upper = grp < n_grp - 1

    barrier = pltpu.get_barrier_semaphore()

    def greet(k, carry):
        pl.semaphore_signal(
            barrier, inc=1, device_id=(grp, lax.rem(sub + k, n_sub)), device_id_type=MESH
        )
        return carry

    lax.fori_loop(1, n_sub, greet, 0)

    @pl.when(has_lower)
    def _():
        pl.semaphore_signal(barrier, inc=1, device_id=(grp - 1, sub), device_id_type=MESH)

    @pl.when(has_upper)
    def _():
        pl.semaphore_signal(barrier, inc=1, device_id=(grp + 1, sub), device_id_type=MESH)

    part_rows = BLK // PARTS
    loads = [
        pltpu.make_async_copy(
            a_hbm.at[pl.ds(i * part_rows, part_rows)],
            a_v.at[pl.ds(i * part_rows, part_rows)],
            a_sem.at[i],
        )
        for i in range(PARTS)
    ]
    for load in loads:
        load.start()

    for c in range(CHUNKS):
        zs[c * NV:(c + 1) * NV, :] = z_ref[:, c * LANES:(c + 1) * LANES]
    source = lax.broadcasted_iota(jnp.int32, (LANES, LANES), 0)
    target = lax.broadcasted_iota(jnp.int32, (LANES, LANES), 1)
    for half in range(2):
        pick = (source == half * BS + lax.rem(target, BS)).astype(F32).astype(BF16)
        moved = jnp.dot(zs[...], pick, preferred_element_type=F32).astype(BF16)
        xn[:, half] = moved.reshape(CHUNKS, NV, LANES)
    for r in range(4):
        for c in range(SEND):
            node = send_s[0, r, c]
            out_b[r, c] = xn[lax.shift_right_logical(node, 1), lax.bitwise_and(node, 1)]

    pl.semaphore_wait(
        barrier, n_sub - 1 + has_lower.astype(jnp.int32) + has_upper.astype(jnp.int32)
    )

    def ghost_copy(r, device):
        return pltpu.make_async_remote_copy(
            src_ref=out_b.at[r], dst_ref=ghost.at[r], send_sem=ghost_send.at[r],
            recv_sem=ghost_recv.at[r], device_id=device, device_id_type=MESH,
        )

    to_next = ghost_copy(0, (grp, following))
    to_prev = ghost_copy(1, (grp, previous))
    to_upper = ghost_copy(2, (lax.rem(grp + 1, n_grp), sub))
    to_lower = ghost_copy(3, (lax.rem(grp + n_grp - 1, n_grp), sub))
    to_next.start()
    to_prev.start()

    @pl.when(has_upper)
    def _():
        to_upper.start()

    @pl.when(has_lower)
    def _():
        to_lower.start()

    @pl.when(jnp.logical_not(has_lower))
    def _():
        ghost[2] = jnp.zeros((SEND, NV, LANES), BF16)

    @pl.when(jnp.logical_not(has_upper))
    def _():
        ghost[3] = jnp.zeros((SEND, NV, LANES), BF16)

    for half in range(2):
        for parity in range(2):
            wanted = half * BS + 2 * target + parity
            pick = jnp.logical_and(source == wanted, target < BS // 2).astype(F32).astype(BF16)
            moved = jnp.dot(zs[...], pick, preferred_element_type=F32).astype(BF16)
            zl[:, half, parity * NV:(parity + 1) * NV] = moved.reshape(CHUNKS, NV, LANES)

    diag_sum = jnp.zeros((2 * NV, NV), F32)
    rhs_sum = jnp.zeros((NV, LANES), F32)
    for c in range(CHUNKS):
        z_c = z_ref[:, c * LANES:(c + 1) * LANES]
        z_f = z_c.astype(F32)
        diag_sum = diag_sum + dot_nt(hi_lo(z_f * diag_ref[c:c + 1, :]), z_c)
        rhs_sum = rhs_sum + z_f * res_ref[c:c + 1, :]
    rhs = jnp.sum(rhs_sum, axis=1, keepdims=True) * (1.0 / 64.0)

    low_half = lax.broadcasted_iota(jnp.int32, (NV, LANES), 1) < BS
    live = live_s[0]
    acc_own[...] = diag_sum
    acc_ghost[...] = jnp.zeros_like(acc_ghost)

    def turn_own(g, carry):
        base = pl.multiple_of(g * GROUP, GROUP)
        for m in range(BS // 2):
            slab = a_v[pl.ds(base, GROUP), m * LANES:(m + 1) * LANES].astype(F32)
            wide[pl.ds(m, GROUP, stride=BS // 2), :] = slab
        own_q = []
        own_x = []
        for t in range(GROUP):
            row = rows_s[0, base + t]
            left = zl[lax.shift_right_logical(row, 1), lax.bitwise_and(row, 1)][:, :BS // 2]
            block = wide[t * (BS // 2):(t + 1) * (BS // 2), :].astype(BF16)
            both = jnp.dot(left, block, preferred_element_type=F32)
            q = jnp.where(low_half, both[:NV], both[NV:])
            q = q * (base + t < live).astype(F32)
            q = hi_lo(q)
            if t % 2 == 0:
                col = cols_s[0, base + t]
                own_q.append(q)
                own_x.append(xn[lax.shift_right_logical(col, 1), lax.bitwise_and(col, 1)])
            else:
                qs[g, t // 2] = q
        acc_own[...] += dot_nt(
            jnp.concatenate(own_q, axis=1), jnp.concatenate(own_x, axis=1)
        )
        return carry

    turns = TURNS // PARTS
    for i in range(PARTS):
        loads[i].wait()
        lax.fori_loop(i * turns, (i + 1) * turns, turn_own, 0)

    to_next.wait()
    to_prev.wait()

    @pl.when(has_upper)
    def _():
        to_upper.wait_send()

    @pl.when(has_lower)
    def _():
        to_upper.wait_recv()

    @pl.when(has_lower)
    def _():
        to_lower.wait_send()

    @pl.when(has_upper)
    def _():
        to_lower.wait_recv()

    def turn_ghost(h, carry):
        for r in range(4):
            q_list = []
            x_list = []
            for e in range(2):
                g = 2 * h + e
                for t in (2 * r + 1, 2 * r + 9):
                    col = lax.bitwise_and(cols_s[0, g * GROUP + t], SEND - 1)
                    q_list.append(qs[g, t // 2])
                    x_list.append(ghost[r, col])
            acc_ghost[r] += dot_nt(
                jnp.concatenate(q_list, axis=1), jnp.concatenate(x_list, axis=1)
            )
        return carry

    lax.fori_loop(0, TURNS // 2, turn_ghost, 0)

    scale = 1.0 / ROWS
    coarse = [(acc_own[:NV] + acc_own[NV:]) * scale]
    for r in range(4):
        coarse.append((acc_ghost[r, :NV] + acc_ghost[r, NV:]) * scale)
    zero = jnp.zeros((NV, NV), F32)
    own, before, after = coarse[:3]
    flipped = jnp.transpose(jnp.concatenate([own, before, after, zero], axis=1))
    strip[:, :LANES] = jnp.concatenate(
        [
            (own + flipped[:NV]) * 0.5,
            before * 0.5,
            after * 0.5,
            jnp.broadcast_to(rhs, (NV, NV)),
        ],
        axis=1,
    )
    strip[:, LANES:] = jnp.concatenate(
        [zero, flipped[2 * NV:3 * NV] * 0.5, flipped[NV:2 * NV] * 0.5, zero], axis=1
    )

    def strip_copy(k, owner):
        return pltpu.make_async_remote_copy(
            src_ref=strip, dst_ref=strips.at[owner], send_sem=strip_send.at[k],
            recv_sem=strip_recv.at[owner], device_id=(grp, lax.rem(sub + k, n_sub)),
            device_id_type=MESH,
        )

    def send(k, carry):
        strip_copy(k, sub).start()
        return carry

    lax.fori_loop(1, n_sub, send, 0)
    strips[sub] = strip[...]
    for o in range(5):
        blocks[o * NV:(o + 1) * NV, :] = jnp.concatenate([coarse[o]] * 4, axis=1)

    def finish(k, carry):
        strip_copy(k, sub).wait_send()
        strip_copy(k, lax.rem(sub + n_sub - k, n_sub)).wait_recv()
        return carry

    lax.fori_loop(1, n_sub, finish, 0)


def eliminate(work):
    sub_row = lax.broadcasted_iota(jnp.int32, (1, NV, LANES), 1)
    for k in range(NV):
        row = work[:, k:k + 1, :]
        row = row * (1.0 / work[:, k:k + 1, k:k + 1])
        work = jnp.where(sub_row == k, row, work - work[:, :, k:k + 1] * row)
    return work


def dot_exact(a, b):
    return jnp.dot(a, b, precision=HIGHEST_PREC, preferred_element_type=F32)


def solve_blocks(systems):
    count = len(systems)
    if count == 1:
        return [eliminate(systems[0][None])[0][:, 3 * NV:]]
    odd = eliminate(jnp.stack(systems[1::2]))
    half = count // 2
    reduced = []
    zero = jnp.zeros((NV, NV), F32)
    for i in range(half):
        even = systems[2 * i]
        ahead, behind = odd[i], odd[(i - 1) % half]
        to_next, to_prev = even[:, 2 * NV:3 * NV], even[:, NV:2 * NV]
        if count == 2:
            gone = dot_exact(to_next + to_prev, ahead)
            link = gone[:, NV:2 * NV] + gone[:, 2 * NV:3 * NV]
            reduced.append(even - jnp.concatenate([link, zero, zero, gone[:, 3 * NV:]], axis=1))
            continue
        up = dot_exact(to_next, ahead)
        down = dot_exact(to_prev, behind)
        diag = even[:, :NV] - up[:, NV:2 * NV] - down[:, 2 * NV:3 * NV]
        right = even[:, 3 * NV:] - up[:, 3 * NV:] - down[:, 3 * NV:]
        reduced.append(
            jnp.concatenate([diag, -down[:, NV:2 * NV], -up[:, 2 * NV:3 * NV], right], axis=1)
        )
    evens = solve_blocks(reduced)
    solved = []
    for i in range(half):
        left, right = evens[i], evens[(i + 1) % half]
        gone = dot_exact(odd[i][:, NV:2 * NV], left) + dot_exact(odd[i][:, 2 * NV:3 * NV], right)
        solved += [left, odd[i][:, 3 * NV:] - gone]
    return solved


def solve_kernel(n_sub, strips, blocks, z_ref, corr, rows_out, found):
    systems = []
    lane = lax.broadcasted_iota(jnp.int32, (NV, LANES), 1)
    for s in range(n_sub):
        near = jnp.where(
            lane < 2 * NV, strips[(s - 1) % n_sub, :, LANES:], strips[(s + 1) % n_sub, :, LANES:]
        )
        systems.append(strips[s, :, :LANES] + near)
    solved = solve_blocks(systems)
    for s in range(n_sub):
        found[s] = jnp.concatenate([solved[s]] * 4, axis=1)
    own = found[lax.axis_index("sub")]
    for c in range(CHUNKS):
        z_c = z_ref[:, c * LANES:(c + 1) * LANES].astype(F32)
        corr[c:c + 1, :] = jnp.sum(z_c * own, axis=0, keepdims=True)
    lane8 = lax.broadcasted_iota(jnp.int32, (8, LANES), 1)
    for o in range(5):
        total = blocks[pl.ds(o * NV, 8, stride=4), :]
        for q in range(1, 4):
            total = jnp.where(
                lane8 >= q * NV, blocks[pl.ds(o * NV + q, 8, stride=4), :], total
            )
        rows_out[o * 8:(o + 1) * 8, :] = total


def per_device(
    n_grp, n_sub, deflation, operator_blocks, diagonal, block_rows, block_cols, live_count,
    send_blocks, residual,
):
    vmem = pl.BlockSpec(memory_space=pltpu.VMEM)
    smem = pl.BlockSpec(memory_space=pltpu.SMEM)
    strips, blocks = pl.pallas_call(
        functools.partial(assemble_kernel, n_grp, n_sub),
        out_shape=(
            jax.ShapeDtypeStruct((n_sub, NV, 2 * LANES), F32),
            jax.ShapeDtypeStruct((5 * NV, LANES), F32),
        ),
        in_specs=[smem] * 4 + [vmem] * 3 + [pl.BlockSpec(memory_space=pl.ANY)],
        out_specs=(vmem, vmem),
        scratch_shapes=[
            pltpu.VMEM((BLK, BS * BS), BF16),
            pltpu.VMEM((CHUNKS * NV, LANES), BF16),
            pltpu.VMEM((CHUNKS, 2, 2 * NV, LANES), BF16),
            pltpu.VMEM((CHUNKS, 2, NV, LANES), BF16),
            pltpu.VMEM((4, SEND, NV, LANES), BF16),
            pltpu.VMEM((4, SEND, NV, LANES), BF16),
            pltpu.VMEM((GROUP * BS // 2, LANES), F32),
            pltpu.VMEM((TURNS, GROUP // 2, 2 * NV, LANES), BF16),
            pltpu.VMEM((NV, 2 * LANES), F32),
            pltpu.VMEM((2 * NV, NV), F32),
            pltpu.VMEM((4, 2 * NV, NV), F32),
            pltpu.SemaphoreType.DMA((PARTS,)),
            pltpu.SemaphoreType.DMA((4,)),
            pltpu.SemaphoreType.DMA((4,)),
            pltpu.SemaphoreType.DMA((n_sub,)),
            pltpu.SemaphoreType.DMA((n_sub,)),
        ],
        compiler_params=pltpu.CompilerParams(
            collective_id=0, has_side_effects=True, vmem_limit_bytes=40 * 2**20
        ),
    )(
        block_rows, block_cols, live_count, send_blocks, deflation,
        diagonal.reshape(CHUNKS, LANES), residual.reshape(CHUNKS, LANES), operator_blocks,
    )
    correction, coarse_rows = pl.pallas_call(
        functools.partial(solve_kernel, n_sub),
        out_shape=(
            jax.ShapeDtypeStruct((CHUNKS, LANES), F32),
            jax.ShapeDtypeStruct((5 * NV * NV // LANES, LANES), F32),
        ),
        in_specs=[vmem] * 3,
        out_specs=(vmem, vmem),
        scratch_shapes=[pltpu.VMEM((n_sub, NV, LANES), F32)],
        compiler_params=pltpu.CompilerParams(vmem_limit_bytes=40 * 2**20),
    )(strips, blocks, deflation)
    return correction.reshape(ROWS), coarse_rows.reshape(1, 5 * NV * NV)


def solution(mesh):
    placed = (
        P(None, ("grp", "sub")),
        P(("grp", "sub"), None),
        P(("grp", "sub")),
        P(("grp", "sub"), None),
        P(("grp", "sub"), None),
        P(("grp", "sub")),
        P(("grp", "sub"), None, None),
        P(("grp", "sub")),
    )
    return jax.shard_map(
        functools.partial(per_device, mesh.shape["grp"], mesh.shape["sub"]),
        mesh=mesh,
        in_specs=placed,
        out_specs=(P(("grp", "sub")), P(("grp", "sub"), None)),
        check_vma=False,
    )
```

time: 234 us -> 48.9 us (0.21)
  the two profiles are of different devices: /device:TPU:4 before, /device:TPU:0 now
where the time goes in v1:
time: 48.9 us; the launch traced here: 48.5 us
  Pallas kernels  40.9 us (84%)
  local copies, waits for them, and re-layouts  6.31 us (13%)
  between operations  1.31 us (3%)
    pallas_call x1, Pallas kernels, per_device(): pl.pallas_call(functools.partial(assemble_kernel, n_grp, n_sub), out_shap...  27.2 us
    pallas_call x1, Pallas kernels, per_device(): pl.pallas_call(functools.partial(solve_kernel, n_sub), out_shape=(jax.Sha...  13.7 us
    unnamed x16, local copies, waits for them, and re-layouts  6.31 us

profile of v1, /device:TPU:0, one launch (start us, length us, event | category | flops | bytes accessed | tf_op | source)
XLA Modules:
  0.0 48.5 jit_solution(17057833085862522927)
XLA Ops:
  1.3 0.0 copy-start
  1.3 1.9 %copy-done = bf16[384,4096]{1,0:T(8,128)(2,1)S(1)} copy-done((bf16[384,4096]{1,0:T(8,128)(2,1)S(1)}, bf16[384,4096]{1,0:T(8,128)(2,1)}, u32[]{:S(2)}) %copy-start) | copy-done | bytes 3145752
  3.2 0.0 copy-start.1
  3.2 0.9 %copy-done.1 = bf16[32,4096]{1,0:T(8,128)(2,1)S(1)} copy-done((bf16[32,4096]{1,0:T(8,128)(2,1)S(1)}, bf16[32,4096]{1,0:T(8,128)(2,1)}, u32[]{:S(2)}) %copy-start.1) | copy-done | bytes 262168
  4.1 0.0 copy-start.3
  4.1 0.7 %copy-done.3 = f32[4096]{0:T(1024)S(1)} copy-done((f32[4096]{0:T(1024)S(1)}, f32[4096]{0:T(1024)}, u32[]{:S(2)}) %copy-start.3) | copy-done | bytes 16408
  4.8 0.0 copy-start.4
  4.8 0.7 %copy-done.4 = f32[4096]{0:T(1024)S(1)} copy-done((f32[4096]{0:T(1024)S(1)}, f32[4096]{0:T(1024)}, u32[]{:S(2)}) %copy-start.4) | copy-done | bytes 16408
  5.6 0.0 copy-start.5
  5.6 0.7 %copy-done.5 = s32[1,4,16]{2,1,0:T(4,128)S(1)} copy-done((s32[1,4,16]{2,1,0:T(4,128)S(1)}, s32[1,4,16]{2,1,0:T(4,128)}, u32[]{:S(2)}) %copy-start.5) | copy-done | bytes 280
  6.2 0.0 copy-start.6
  6.2 0.7 %copy-done.6 = s32[1,384]{1,0:T(1,128)S(1)} copy-done((s32[1,384]{1,0:T(1,128)S(1)}, s32[1,384]{1,0:T(1,128)}, u32[]{:S(2)}) %copy-start.6) | copy-done | bytes 1560
  6.9 0.0 copy-start.7
  6.9 0.7 %copy-done.7 = s32[1,384]{1,0:T(1,128)S(1)} copy-done((s32[1,384]{1,0:T(1,128)S(1)}, s32[1,384]{1,0:T(1,128)}, u32[]{:S(2)}) %copy-start.7) | copy-done | bytes 1560
  7.6 0.0 copy-start.2
  7.6 27.2 %shard_map.95 = (f32[8,32,256]{2,1,0:T(8,128)S(1)}, f32[160,128]{1,0:T(8,128)S(1)}) custom-call(s32[1,384]{1,0:T(1,128)S(1)} %copy-done.6, s32[1,384]{1,0:T(1,128)S(1)} %copy-done.7, s32[1]{0:T(128)S(6)} %copy.10.live_s, s32[1,4,16]{2,1,0:T(4,128)S(1)} %copy-done.5, bf16[32,4096]{1,0:T(8,128)(2,1)S(1)} %copy-done.1, f32[32,128]{1,0:T(8,128)S(1)} %bitcast.4, ...), custom_call_target="tpu_custom_call" | custom-call | tf_op jit(solution)/shard_map/pallas_call | solution.py:337
  34.8 0.0 copy-done.2
  34.9 13.7 %shard_map.96 = (f32[32,128]{1,0:T(8,128)}, f32[40,128]{1,0:T(8,128)}) custom-call(f32[8,32,256]{2,1,0:T(8,128)S(1)} %get-tuple-element.6.strips, f32[160,128]{1,0:T(8,128)S(1)} %get-tuple-element.7.blocks, bf16[32,4096]{1,0:T(8,128)(2,1)S(1)} %copy-done.2), custom_call_target="tpu_custom_call" | custom-call | tf_op jit(solution)/shard_map/pallas_call | solution.py:370
Async XLA Ops:
  1.3 1.9 %copy-start = (bf16[384,4096]{1,0:T(8,128)(2,1)S(1)}, bf16[384,4096]{1,0:T(8,128)(2,1)}, u32[]{:S(2)}) copy-start(bf16[384,4096]{1,0:T(8,128)(2,1)} %a_hbm.1) | copy-start | bytes 9437188
  3.2 0.9 %copy-start.1 = (bf16[32,4096]{1,0:T(8,128)(2,1)S(1)}, bf16[32,4096]{1,0:T(8,128)(2,1)}, u32[]{:S(2)}) copy-start(bf16[32,4096]{1,0:T(8,128)(2,1)} %z_ref.3) | copy-start | bytes 786436
  4.1 0.7 %copy-start.3 = (f32[4096]{0:T(1024)S(1)}, f32[4096]{0:T(1024)}, u32[]{:S(2)}) copy-start(f32[4096]{0:T(1024)} %param.10) | copy-start | bytes 49156
  4.8 0.7 %copy-start.4 = (f32[4096]{0:T(1024)S(1)}, f32[4096]{0:T(1024)}, u32[]{:S(2)}) copy-start(f32[4096]{0:T(1024)} %param.15) | copy-start | bytes 49156
  5.6 0.7 %copy-start.5 = (s32[1,4,16]{2,1,0:T(4,128)S(1)}, s32[1,4,16]{2,1,0:T(4,128)}, u32[]{:S(2)}) copy-start(s32[1,4,16]{2,1,0:T(4,128)} %send_s.1) | copy-start | bytes 772
  6.2 0.7 %copy-start.6 = (s32[1,384]{1,0:T(1,128)S(1)}, s32[1,384]{1,0:T(1,128)}, u32[]{:S(2)}) copy-start(s32[1,384]{1,0:T(1,128)} %rows_s.1) | copy-start | bytes 4612
  6.9 0.7 %copy-start.7 = (s32[1,384]{1,0:T(1,128)S(1)}, s32[1,384]{1,0:T(1,128)}, u32[]{:S(2)}) copy-start(s32[1,384]{1,0:T(1,128)} %cols_s.1) | copy-start | bytes 4612
  7.6 27.2 %copy-start.2 = (bf16[32,4096]{1,0:T(8,128)(2,1)S(1)}, bf16[32,4096]{1,0:T(8,128)(2,1)}, u32[]{:S(2)}) copy-start(bf16[32,4096]{1,0:T(8,128)(2,1)} %z_ref.3) | copy-start | bytes 786436

commit v2 on v1

--- a/solution.py
+++ b/solution.py
@@ -18,6 +18,7 @@
 GROUP = 16
 TURNS = BLK // GROUP
 PARTS = 4
+PIVOTS = 4
 
 HIGHEST_PREC = lax.Precision.HIGHEST
 MESH = pl.DeviceIdType.MESH
@@ -37,9 +38,9 @@
 
 def assemble_kernel(
     n_grp, n_sub,
-    rows_s, cols_s, live_s, send_s, z_ref, diag_ref, res_ref, a_hbm,
+    live_s, rows_h, cols_h, send_h, z_h, diag_h, res_h, a_hbm,
     strips, blocks,
-    a_v, zs, zl, xn, out_b, ghost, wide, qs, strip, acc_own, acc_ghost,
+    rows_s, cols_s, send_s, z_ref, diag_ref, res_ref, in_sem, a_v, zs, zl, xn, out_b, ghost, wide, qs, strip, acc_own, acc_ghost,
     a_sem, ghost_send, ghost_recv, strip_send, strip_recv,
 ):
     grp = lax.axis_index("grp")
@@ -49,6 +50,15 @@
     has_lower = grp > 0
     has_upper = grp < n_grp - 1
 
+    pairs = [
+        (z_h, z_ref), (send_h, send_s), (rows_h, rows_s), (cols_h, cols_s), (diag_h, diag_ref),
+        (res_h, res_ref),
+    ]
+    inputs = [
+        pltpu.make_async_copy(held, here, in_sem.at[i]) for i, (held, here) in enumerate(pairs)
+    ]
+    for copy in inputs:
+        copy.start()
     barrier = pltpu.get_barrier_semaphore()
 
     def greet(k, carry):
@@ -78,6 +88,8 @@
     ]
     for load in loads:
         load.start()
+
+    inputs[0].wait()
 
     for c in range(CHUNKS):
         zs[c * NV:(c + 1) * NV, :] = z_ref[:, c * LANES:(c + 1) * LANES]
@@ -87,6 +99,7 @@
         pick = (source == half * BS + lax.rem(target, BS)).astype(F32).astype(BF16)
         moved = jnp.dot(zs[...], pick, preferred_element_type=F32).astype(BF16)
         xn[:, half] = moved.reshape(CHUNKS, NV, LANES)
+    inputs[1].wait()
     for r in range(4):
         for c in range(SEND):
             node = send_s[0, r, c]
@@ -131,6 +144,9 @@
             pick = jnp.logical_and(source == wanted, target < BS // 2).astype(F32).astype(BF16)
             moved = jnp.dot(zs[...], pick, preferred_element_type=F32).astype(BF16)
             zl[:, half, parity * NV:(parity + 1) * NV] = moved.reshape(CHUNKS, NV, LANES)
+
+    for copy in inputs[2:]:
+        copy.wait()
 
     diag_sum = jnp.zeros((2 * NV, NV), F32)
     rhs_sum = jnp.zeros((NV, LANES), F32)
@@ -258,11 +274,28 @@
 
 
 def eliminate(work):
-    sub_row = lax.broadcasted_iota(jnp.int32, (1, NV, LANES), 1)
-    for k in range(NV):
-        row = work[:, k:k + 1, :]
-        row = row * (1.0 / work[:, k:k + 1, k:k + 1])
-        work = jnp.where(sub_row == k, row, work - work[:, :, k:k + 1] * row)
+    row_of = lax.broadcasted_iota(jnp.int32, (1, NV, LANES), 1)
+    for k in range(0, NV, PIVOTS):
+        span = range(PIVOTS)
+        cols = [jnp.broadcast_to(work[:, :, k + j:k + j + 1], work.shape) for j in span]
+        small = [[cols[j][:, k + i:k + i + 1, :] for j in span] for i in span]
+        rows = [work[:, k + i:k + i + 1, :] for i in span]
+        for i in span:
+            inverse = 1.0 / small[i][i]
+            rows[i] = rows[i] * inverse
+            for j in range(i + 1, PIVOTS):
+                small[i][j] = small[i][j] * inverse
+            for l in span:
+                if l != i:
+                    rows[l] = rows[l] - small[l][i] * rows[i]
+                    for j in range(i + 1, PIVOTS):
+                        small[l][j] = small[l][j] - small[l][i] * small[i][j]
+        rest = work
+        for j in span:
+            rest = rest - cols[j] * rows[j]
+        for i in span:
+            rest = jnp.where(row_of == k + i, rows[i], rest)
+        work = rest
     return work
 
 
@@ -333,16 +366,23 @@
     send_blocks, residual,
 ):
     vmem = pl.BlockSpec(memory_space=pltpu.VMEM)
-    smem = pl.BlockSpec(memory_space=pltpu.SMEM)
     strips, blocks = pl.pallas_call(
         functools.partial(assemble_kernel, n_grp, n_sub),
         out_shape=(
             jax.ShapeDtypeStruct((n_sub, NV, 2 * LANES), F32),
             jax.ShapeDtypeStruct((5 * NV, LANES), F32),
         ),
-        in_specs=[smem] * 4 + [vmem] * 3 + [pl.BlockSpec(memory_space=pl.ANY)],
+        in_specs=[pl.BlockSpec(memory_space=pltpu.SMEM)]
+        + [pl.BlockSpec(memory_space=pltpu.HBM)] * 7,
         out_specs=(vmem, vmem),
         scratch_shapes=[
+            pltpu.SMEM((1, BLK), jnp.int32),
+            pltpu.SMEM((1, BLK), jnp.int32),
+            pltpu.SMEM((1, 4, SEND), jnp.int32),
+            pltpu.VMEM((NV, ROWS), BF16),
+            pltpu.VMEM((CHUNKS, LANES), F32),
+            pltpu.VMEM((CHUNKS, LANES), F32),
+            pltpu.SemaphoreType.DMA((6,)),
             pltpu.VMEM((BLK, BS * BS), BF16),
             pltpu.VMEM((CHUNKS * NV, LANES), BF16),
             pltpu.VMEM((CHUNKS, 2, 2 * NV, LANES), BF16),
@@ -364,8 +404,14 @@
             collective_id=0, has_side_effects=True, vmem_limit_bytes=40 * 2**20
         ),
     )(
-        block_rows, block_cols, live_count, send_blocks, deflation,
-        diagonal.reshape(CHUNKS, LANES), residual.reshape(CHUNKS, LANES), operator_blocks,
+        live_count,
+        *[
+            pltpu.with_memory_space_constraint(held, pltpu.HBM)
+            for held in (
+                block_rows, block_cols, send_blocks, deflation,
+                diagonal.reshape(CHUNKS, LANES), residual.reshape(CHUNKS, LANES), operator_blocks,
+            )
+        ],
     )
     correction, coarse_rows = pl.pallas_call(
         functools.partial(solve_kernel, n_sub),

time: 48.9 us -> 36.7 us (0.75)
  local copies, waits for them, and re-layouts: 6.31 us -> 0.01 us
  Pallas kernels: 40.9 us -> 35.2 us
    unnamed x16 -> x2, local copies, waits for them, and re-layouts: 6.31 us -> 0.01 us
    pallas_call x1, Pallas kernels: 13.7 us -> 8.58 us  [per_device(): pl.pallas_call(functools.partial(solve_kernel, n_sub), out_shape=(jax.Sha...]
    pallas_call x1, Pallas kernels: 27.2 us -> 26.7 us  [per_device(): pl.pallas_call(functools.partial(assemble_kernel, n_grp, n_sub), out_shap...]
where the time goes in v2:
time: 36.7 us; the launch traced here: 36.6 us
  Pallas kernels  35.2 us (96%)
  between operations  1.35 us (4%)
    pallas_call x1, Pallas kernels, per_device(): pl.pallas_call(functools.partial(assemble_kernel, n_grp, n_sub), out_shap...  26.7 us
    pallas_call x1, Pallas kernels, per_device(): pl.pallas_call(functools.partial(solve_kernel, n_sub), out_shape=(jax.Sha...  8.58 us

profile of v2, /device:TPU:0, one launch (start us, length us, event | category | flops | bytes accessed | tf_op | source)
XLA Modules:
  0.0 36.6 jit_solution(16469294822982457177)
XLA Ops:
  0.6 0.0 copy-start
  1.3 26.7 %shard_map.95 = (f32[8,32,256]{2,1,0:T(8,128)S(1)}, f32[160,128]{1,0:T(8,128)S(1)}) custom-call(s32[1]{0:T(128)S(6)} %copy.10.live_s, s32[1,384]{1,0:T(1,128)} %rows_h.1, s32[1,384]{1,0:T(1,128)} %cols_h.1, s32[1,4,16]{2,1,0:T(4,128)} %send_h.1, bf16[32,4096]{1,0:T(8,128)(2,1)} %z_ref.1, f32[32,128]{1,0:T(8,128)} %bitcast.4, f32[32,128]{1,0:T(8,128)} %bitcast.5, ...), custom_call_target="tpu_custom_call" | custom-call | tf_op jit(solution)/shard_map/pallas_call | solution.py:369
  28.0 0.0 copy-done
  28.0 8.6 %shard_map.96 = (f32[32,128]{1,0:T(8,128)}, f32[40,128]{1,0:T(8,128)}) custom-call(f32[8,32,256]{2,1,0:T(8,128)S(1)} %get-tuple-element.6.strips, f32[160,128]{1,0:T(8,128)S(1)} %get-tuple-element.7.blocks, bf16[32,4096]{1,0:T(8,128)(2,1)S(1)} %copy-done), custom_call_target="tpu_custom_call" | custom-call | tf_op jit(solution)/shard_map/pallas_call | solution.py:416
Async XLA Ops:
  0.6 27.4 %copy-start = (bf16[32,4096]{1,0:T(8,128)(2,1)S(1)}, bf16[32,4096]{1,0:T(8,128)(2,1)}, u32[]{:S(2)}) copy-start(bf16[32,4096]{1,0:T(8,128)(2,1)} %z_ref.1) | copy-start | bytes 786436

commit v3 on v2

--- a/solution.py
+++ b/solution.py
@@ -19,6 +19,7 @@
 TURNS = BLK // GROUP
 PARTS = 4
 PIVOTS = 4
+PITCH = 40
 
 HIGHEST_PREC = lax.Precision.HIGHEST
 MESH = pl.DeviceIdType.MESH
@@ -166,13 +167,13 @@
         base = pl.multiple_of(g * GROUP, GROUP)
         for m in range(BS // 2):
             slab = a_v[pl.ds(base, GROUP), m * LANES:(m + 1) * LANES].astype(F32)
-            wide[pl.ds(m, GROUP, stride=BS // 2), :] = slab
+            wide[pl.ds(m, GROUP, stride=PITCH), :] = slab
         own_q = []
         own_x = []
         for t in range(GROUP):
             row = rows_s[0, base + t]
             left = zl[lax.shift_right_logical(row, 1), lax.bitwise_and(row, 1)][:, :BS // 2]
-            block = wide[t * (BS // 2):(t + 1) * (BS // 2), :].astype(BF16)
+            block = wide[t * PITCH:t * PITCH + BS // 2, :].astype(BF16)
             both = jnp.dot(left, block, preferred_element_type=F32)
             q = jnp.where(low_half, both[:NV], both[NV:])
             q = q * (base + t < live).astype(F32)
@@ -233,20 +234,15 @@
     coarse = [(acc_own[:NV] + acc_own[NV:]) * scale]
     for r in range(4):
         coarse.append((acc_ghost[r, :NV] + acc_ghost[r, NV:]) * scale)
-    zero = jnp.zeros((NV, NV), F32)
     own, before, after = coarse[:3]
-    flipped = jnp.transpose(jnp.concatenate([own, before, after, zero], axis=1))
-    strip[:, :LANES] = jnp.concatenate(
+    strip[...] = jnp.concatenate(
         [
-            (own + flipped[:NV]) * 0.5,
+            (own + jnp.transpose(own)) * 0.5,
             before * 0.5,
             after * 0.5,
             jnp.broadcast_to(rhs, (NV, NV)),
         ],
         axis=1,
-    )
-    strip[:, LANES:] = jnp.concatenate(
-        [zero, flipped[2 * NV:3 * NV] * 0.5, flipped[NV:2 * NV] * 0.5, zero], axis=1
     )
 
     def strip_copy(k, owner):
@@ -338,12 +334,12 @@
 
 def solve_kernel(n_sub, strips, blocks, z_ref, corr, rows_out, found):
     systems = []
-    lane = lax.broadcasted_iota(jnp.int32, (NV, LANES), 1)
+    zero = jnp.zeros((NV, NV), F32)
+    flipped = [jnp.transpose(strips[s]) for s in range(n_sub)]
     for s in range(n_sub):
-        near = jnp.where(
-            lane < 2 * NV, strips[(s - 1) % n_sub, :, LANES:], strips[(s + 1) % n_sub, :, LANES:]
-        )
-        systems.append(strips[s, :, :LANES] + near)
+        from_prev = flipped[(s - 1) % n_sub][2 * NV:3 * NV]
+        from_next = flipped[(s + 1) % n_sub][NV:2 * NV]
+        systems.append(strips[s] + jnp.concatenate([zero, from_prev, from_next, zero], axis=1))
     solved = solve_blocks(systems)
     for s in range(n_sub):
         found[s] = jnp.concatenate([solved[s]] * 4, axis=1)
@@ -369,7 +365,7 @@
     strips, blocks = pl.pallas_call(
         functools.partial(assemble_kernel, n_grp, n_sub),
         out_shape=(
-            jax.ShapeDtypeStruct((n_sub, NV, 2 * LANES), F32),
+            jax.ShapeDtypeStruct((n_sub, NV, LANES), F32),
             jax.ShapeDtypeStruct((5 * NV, LANES), F32),
         ),
         in_specs=[pl.BlockSpec(memory_space=pltpu.SMEM)]
@@ -389,9 +385,9 @@
             pltpu.VMEM((CHUNKS, 2, NV, LANES), BF16),
             pltpu.VMEM((4, SEND, NV, LANES), BF16),
             pltpu.VMEM((4, SEND, NV, LANES), BF16),
-            pltpu.VMEM((GROUP * BS // 2, LANES), F32),
+            pltpu.VMEM((GROUP * PITCH, LANES), F32),
             pltpu.VMEM((TURNS, GROUP // 2, 2 * NV, LANES), BF16),
-            pltpu.VMEM((NV, 2 * LANES), F32),
+            pltpu.VMEM((NV, LANES), F32),
             pltpu.VMEM((2 * NV, NV), F32),
             pltpu.VMEM((4, 2 * NV, NV), F32),
             pltpu.SemaphoreType.DMA((PARTS,)),

time: 36.7 us -> 32.3 us (0.88)
  Pallas kernels: 35.2 us -> 30.8 us
    pallas_call x1, Pallas kernels: 26.7 us -> 21.9 us  [per_device(): pl.pallas_call(functools.partial(assemble_kernel, n_grp, n_sub), out_shap...]
where the time goes in v3:
time: 32.3 us; the launch traced here: 32.1 us
  Pallas kernels  30.8 us (95%)
  between operations  1.35 us (4%)
    pallas_call x1, Pallas kernels, per_device(): pl.pallas_call(functools.partial(assemble_kernel, n_grp, n_sub), out_shap...  21.9 us
    pallas_call x1, Pallas kernels, per_device(): pl.pallas_call(functools.partial(solve_kernel, n_sub), out_shape=(jax.Sha...  8.89 us

profile of v3, /device:TPU:0, one launch (start us, length us, event | category | flops | bytes accessed | tf_op | source)
XLA Modules:
  0.0 32.1 jit_solution(343271932033247468)
XLA Ops:
  0.6 0.0 copy-start
  1.3 21.9 %shard_map.95 = (f32[8,32,128]{2,1,0:T(8,128)S(1)}, f32[160,128]{1,0:T(8,128)S(1)}) custom-call(s32[1]{0:T(128)S(6)} %copy.10.live_s, s32[1,384]{1,0:T(1,128)} %rows_h.1, s32[1,384]{1,0:T(1,128)} %cols_h.1, s32[1,4,16]{2,1,0:T(4,128)} %send_h.1, bf16[32,4096]{1,0:T(8,128)(2,1)} %z_ref.1, f32[32,128]{1,0:T(8,128)} %bitcast.4, f32[32,128]{1,0:T(8,128)} %bitcast.5, ...), custom_call_target="tpu_custom_call" | custom-call | tf_op jit(solution)/shard_map/pallas_call | solution.py:365
  23.2 0.0 copy-done
  23.2 8.9 %shard_map.96 = (f32[32,128]{1,0:T(8,128)}, f32[40,128]{1,0:T(8,128)}) custom-call(f32[8,32,128]{2,1,0:T(8,128)S(1)} %get-tuple-element.6.strips, f32[160,128]{1,0:T(8,128)S(1)} %get-tuple-element.7.blocks, bf16[32,4096]{1,0:T(8,128)(2,1)S(1)} %copy-done), custom_call_target="tpu_custom_call" | custom-call | tf_op jit(solution)/shard_map/pallas_call | solution.py:412
Async XLA Ops:
  0.6 22.6 %copy-start = (bf16[32,4096]{1,0:T(8,128)(2,1)S(1)}, bf16[32,4096]{1,0:T(8,128)(2,1)}, u32[]{:S(2)}) copy-start(bf16[32,4096]{1,0:T(8,128)(2,1)} %z_ref.1) | copy-start | bytes 786436

commit v4 on v3

--- a/solution.py
+++ b/solution.py
@@ -189,10 +189,9 @@
         )
         return carry
 
-    turns = TURNS // PARTS
-    for i in range(PARTS):
-        loads[i].wait()
-        lax.fori_loop(i * turns, (i + 1) * turns, turn_own, 0)
+    for load in loads:
+        load.wait()
+    lax.fori_loop(0, TURNS, turn_own, 0)
 
     to_next.wait()
     to_prev.wait()

time: 32.3 us -> 32.3 us (level)
  no operation moved by 1% of the time
where the time goes in v4:
time: 32.3 us; the launch traced here: 32.2 us
  Pallas kernels  30.8 us (95%)
  between operations  1.35 us (4%)
    pallas_call x1, Pallas kernels, per_device(): pl.pallas_call(functools.partial(assemble_kernel, n_grp, n_sub), out_shap...  21.9 us
    pallas_call x1, Pallas kernels, per_device(): pl.pallas_call(functools.partial(solve_kernel, n_sub), out_shape=(jax.Sha...  8.9 us

profile of v4, /device:TPU:0, one launch (start us, length us, event | category | flops | bytes accessed | tf_op | source)
XLA Modules:
  0.0 32.2 jit_solution(6385879742168905330)
XLA Ops:
  0.6 0.0 copy-start
  1.3 21.9 %shard_map.95 = (f32[8,32,128]{2,1,0:T(8,128)S(1)}, f32[160,128]{1,0:T(8,128)S(1)}) custom-call(s32[1]{0:T(128)S(6)} %copy.10.live_s, s32[1,384]{1,0:T(1,128)} %rows_h.1, s32[1,384]{1,0:T(1,128)} %cols_h.1, s32[1,4,16]{2,1,0:T(4,128)} %send_h.1, bf16[32,4096]{1,0:T(8,128)(2,1)} %z_ref.1, f32[32,128]{1,0:T(8,128)} %bitcast.4, f32[32,128]{1,0:T(8,128)} %bitcast.5, ...), custom_call_target="tpu_custom_call" | custom-call | tf_op jit(solution)/shard_map/pallas_call | solution.py:364
  23.3 0.0 copy-done
  23.3 8.9 %shard_map.96 = (f32[32,128]{1,0:T(8,128)}, f32[40,128]{1,0:T(8,128)}) custom-call(f32[8,32,128]{2,1,0:T(8,128)S(1)} %get-tuple-element.6.strips, f32[160,128]{1,0:T(8,128)S(1)} %get-tuple-element.7.blocks, bf16[32,4096]{1,0:T(8,128)(2,1)S(1)} %copy-done), custom_call_target="tpu_custom_call" | custom-call | tf_op jit(solution)/shard_map/pallas_call | solution.py:411
Async XLA Ops:
  0.6 22.6 %copy-start = (bf16[32,4096]{1,0:T(8,128)(2,1)S(1)}, bf16[32,4096]{1,0:T(8,128)(2,1)}, u32[]{:S(2)}) copy-start(bf16[32,4096]{1,0:T(8,128)(2,1)} %z_ref.1) | copy-start | bytes 786436
